TPU v7x, 768 devices: a whole 4x8x12 slice. The times are simulated.
768 devices in a mesh: blk: 48 (over z, x_lo, core), dp: 16 (over y, x_hi).
Axes of the slice: x: 4 (x_hi: 2, x_lo: 2; x = x_hi * 2 + x_lo), y: 8, z: 12, core: 2. Of those that a mesh axis runs over, the one named last changes fastest.
Arguments:
- tokens: bfloat16 [6144, 3072], P('dp'), may hold values from -6 to 6
- cotangent: bfloat16 [6144, 3072], P('dp'), may hold values from -0.59765625 to 0.59765625
- w_gate: bfloat16 [3072, 18432], P(None, 'blk'), may hold values from -0.109375 to 0.109375
- w_up: bfloat16 [3072, 18432], P(None, 'blk'), may hold values from -0.109375 to 0.109375
- w_down_t: bfloat16 [3072, 18432], P(None, 'blk'), may hold values from -0.046875 to 0.046875
- gate_probs: float32 [6144, 2], P('dp'), may hold values from 0.1 to 0.9
- slot_ids: int32 [6144], P('dp'), may hold values from 0 to 1
- block_list: int32 [16, 2], P('dp'), may hold values from 0 to 2, as said below
- block_count: int32 [16], P('dp'), may hold values from 1 to 2, as said below
Outputs:
- grad_tokens: bfloat16 [6144, 3072], P('dp', 'blk')
- grad_probs: float32 [6144, 2], P('dp')
- grad_gate: bfloat16 [3072, 18432], P('dp', 'blk')
- grad_up: bfloat16 [3072, 18432], P('dp', 'blk')
- grad_down_t: bfloat16 [3072, 18432], P('dp', 'blk')
Inputs may be any that keep to these rules, and one draw needn't show every extreme that they name: `block_list`: each row holds 2 different block numbers of the group. `block_count`: in every draw some group has 2 live blocks and another group one.
All inputs are finite; a program needn't handle non-finite values.
Results may differ from a plain program's by a relative error of at most 0.019.
Values may be sent and summed in bfloat16 or wider, within the bound.
A program may use at most 64 MiB of HBM per device.

v0:
```python
import jax
import jax.numpy as jnp
from jax import lax
from jax.sharding import PartitionSpec as P

BLOCK = 128


def contract_lead(left, right):
    return lax.dot_general(
        left, right, (((0,), (0,)), ((), ())), preferred_element_type=jnp.float32
    )


def contract_last(left, right):
    return lax.dot_general(
        left, right, (((1,), (1,)), ((), ())), preferred_element_type=jnp.float32
    )


def body(tokens, cotangent, w_gate, w_up, w_down_t, gate_probs, slot_ids, block_list, block_count):
    blocks = block_list[0]
    filled = block_count[0]
    slot_total = block_list.shape[1]
    offsets = [blocks[which] * BLOCK for which in range(slot_total)]
    rows_in = jnp.concatenate(
        [lax.dynamic_slice_in_dim(tokens, offset, BLOCK, 0) for offset in offsets], axis=0
    )
    rows_cot = jnp.concatenate(
        [lax.dynamic_slice_in_dim(cotangent, offset, BLOCK, 0) for offset in offsets], axis=0
    )
    probs = jnp.concatenate(
        [lax.dynamic_slice_in_dim(gate_probs, offset, BLOCK, 0) for offset in offsets], axis=0
    )
    slots = jnp.concatenate(
        [lax.dynamic_slice_in_dim(slot_ids, offset, BLOCK, 0) for offset in offsets], axis=0
    )
    live = jnp.concatenate(
        [
            jnp.full((BLOCK,), 1.0, jnp.float32) * (which < filled).astype(jnp.float32)
            for which in range(slot_total)
        ]
    )
    gates = jnp.where(slots == 0, probs[:, 0], probs[:, 1])
    pre_gate = jnp.dot(rows_in, w_gate, preferred_element_type=jnp.float32)
    pre_up = jnp.dot(rows_in, w_up, preferred_element_type=jnp.float32)
    sigmoid_gate = jax.nn.sigmoid(pre_gate)
    activated = pre_gate * sigmoid_gate
    hidden = (activated * pre_up).astype(jnp.bfloat16)
    back = jnp.dot(rows_cot, w_down_t, preferred_element_type=jnp.float32)
    partial_dots = jnp.sum(hidden.astype(jnp.float32) * back, axis=1)
    dots = lax.psum(partial_dots, "blk")
    factor = (gates * live)[:, None]
    d_hidden = back * factor
    d_pre_gate = (
        d_hidden * pre_up * sigmoid_gate * (1.0 + pre_gate * (1.0 - sigmoid_gate))
    ).astype(jnp.bfloat16)
    d_pre_up = (d_hidden * activated).astype(jnp.bfloat16)
    scaled_hidden = (hidden.astype(jnp.float32) * factor).astype(jnp.bfloat16)
    input_terms = contract_last(d_pre_gate, w_gate) + contract_last(d_pre_up, w_up)
    rows_grad = lax.psum_scatter(input_terms, "blk", scatter_dimension=1, tiled=True)
    rows_grad = rows_grad.astype(jnp.bfloat16)
    values = dots * live
    columns = jnp.stack(
        [jnp.where(slots == 0, values, 0.0), jnp.where(slots == 1, values, 0.0)], axis=1
    )
    grad_tokens = jnp.zeros((tokens.shape[0], rows_grad.shape[1]), jnp.bfloat16)
    grad_probs = jnp.zeros((tokens.shape[0], 2), jnp.float32)
    for which in range(slot_total):
        grad_tokens = lax.dynamic_update_slice_in_dim(
            grad_tokens, rows_grad[which * BLOCK : (which + 1) * BLOCK], offsets[which], 0
        )
        grad_probs = lax.dynamic_update_slice_in_dim(
            grad_probs, columns[which * BLOCK : (which + 1) * BLOCK], offsets[which], 0
        )
    summed_gate, summed_up, summed_down = (
        lax.psum_scatter(
            contract_lead(rows_in, d_pre_gate).astype(jnp.bfloat16),
            "dp",
            scatter_dimension=0,
            tiled=True,
        ).astype(jnp.float32),
        lax.psum_scatter(
            contract_lead(rows_in, d_pre_up).astype(jnp.bfloat16),
            "dp",
            scatter_dimension=0,
            tiled=True,
        ).astype(jnp.float32),
        lax.psum_scatter(
            contract_lead(rows_cot, scaled_hidden).astype(jnp.bfloat16),
            "dp",
            scatter_dimension=0,
            tiled=True,
        ).astype(jnp.float32),
    )
    return (
        grad_tokens,
        grad_probs,
        summed_gate.astype(jnp.bfloat16),
        summed_up.astype(jnp.bfloat16),
        summed_down.astype(jnp.bfloat16),
    )


def solution(mesh):
    placed = (
        P("dp", None),
        P("dp", None),
        P(None, "blk"),
        P(None, "blk"),
        P(None, "blk"),
        P("dp", None),
        P("dp"),
        P("dp", None),
        P("dp"),
    )
    return jax.shard_map(
        body,
        mesh=mesh,
        in_specs=placed,
        out_specs=(P("dp", "blk"), P("dp", None), P("dp", "blk"), P("dp", "blk"), P("dp", "blk")),
        check_vma=False,
    )
```

profile of v0, /device:TPU:1, one launch (start us, length us, event | category | flops | bytes accessed | tf_op | source)
XLA Modules:
  0.0 892.5 jit_solution(7058308922828017808)
XLA Ops:
  7.2 0.0 copy-start
  7.2 0.0 reduce-scatter.5.cloned.1.call-start
  7.2 1.4 fusion.13
  9.9 0.7 constant_dynamic-slice_fusion.2
  10.6 0.8 fusion.12
  12.1 2.1 constant_dynamic-slice_fusion.1
  14.2 0.0 copy-start.2
  14.2 0.0 copy-start.3
  14.3 0.0 copy-start.4
  14.3 0.0 copy-done
  14.3 0.0 copy-start.1
  14.3 1.0 fusion.10
  15.3 0.0 copy-done.2
  15.3 1.5 copy-done.1
  16.8 0.0 copy-start.8
  16.8 1.0 fusion.11
  17.8 0.0 copy-done.3
  17.9 0.0 copy-done.4
  17.9 0.6 copy-done.8
  18.4 2.4 fusion.1
  20.8 1.0 fusion.14
  21.8 2.6 convolution_add_fusion
  24.5 0.0 reduce-scatter.5.cloned.1.call-update
  24.5 0.0 reduce-scatter.11.cloned.1.call-start
  24.5 3.9 convolution_convert_fusion
  28.5 0.0 reduce-scatter.11.cloned.1.call-update
  28.5 0.0 reduce-scatter.7.cloned.1.call-start
  28.5 3.6 convolution_convert_fusion.2
  32.1 0.0 reduce-scatter.7.cloned.1.call-update
  32.1 0.0 reduce-scatter.9.cloned.1.call-start
  32.2 3.6 convolution_convert_fusion.1
  35.8 0.0 copy-start.7
  35.8 0.0 reduce-scatter.9.cloned.1.call-update
  35.8 0.7 copy-done.7
  36.5 89.6 %psum.7 = f32[256]{0:T(256)S(1)} all-reduce(f32[256]{0:T(256)S(1)} %copy-done.7), channel_id=1, replica_groups=mesh['blk'=48,'dp'=16] {'blk'}, use_global_device_ids=true, to_apply=%region_2.3 | all-reduce | flops 256 | bytes 2048 | tf_op jit(solution)/shard_map/psum | solution.py:52
  126.2 0.0 copy-start.6
  126.2 81.6 %reduce-scatter.5.cloned.1.call-done = f32[256,64]{0,1:T(8,128)} async-done(((f32[256,3072]{0,1:T(8,128)}), f32[256,64]{0,1:T(8,128)}) %reduce-scatter.5.cloned.1.call-update) | async-done | bytes 65552 | tf_op jit(solution)/shard_map/reduce_scatter | solution.py:61
  207.8 0.8 convert_element_type.52
  208.7 0.0 copy-start.5
  208.7 223.5 %reduce-scatter.11.cloned.1.call-done = bf16[192,384]{1,0:T(8,128)(2,1)} async-done(((bf16[3072,384]{1,0:T(8,128)(2,1)}), bf16[192,384]{1,0:T(8,128)(2,1)}) %reduce-scatter.11.cloned.1.call-update) | async-done | bytes 147472 | tf_op jit(solution)/shard_map/reduce_scatter | solution.py:89
  432.2 227.0 %reduce-scatter.7.cloned.1.call-done = bf16[192,384]{1,0:T(8,128)(2,1)} async-done(((bf16[3072,384]{1,0:T(8,128)(2,1)}), bf16[192,384]{1,0:T(8,128)(2,1)}) %reduce-scatter.7.cloned.1.call-update) | async-done | bytes 147472 | tf_op jit(solution)/shard_map/reduce_scatter | solution.py:77
  659.1 226.8 %reduce-scatter.9.cloned.1.call-done = bf16[192,384]{1,0:T(8,128)(2,1)} async-done(((bf16[3072,384]{1,0:T(8,128)(2,1)}), bf16[192,384]{1,0:T(8,128)(2,1)}) %reduce-scatter.9.cloned.1.call-update) | async-done | bytes 147472 | tf_op jit(solution)/shard_map/reduce_scatter | solution.py:83
  885.9 0.0 copy-done.6
  885.9 0.0 copy-done.5
  (10 shorter events, 0.1 us)
Async XLA Ops:
  7.2 7.1 copy-start
  7.2 200.6 %reduce-scatter.5.cloned.1.call-start = ((), (), s32[]{:S(2)}) async-start(), calls=%async_computation.4 | async-start | bytes 3211264 | tf_op jit(solution)/shard_map/reduce_scatter | solution.py:61
  14.2 1.1 copy-start.2
  14.2 3.6 copy-start.3
  14.3 3.6 copy-start.4
  14.3 2.5 copy-start.1
  16.8 1.7 copy-start.8
  24.5 407.7 %reduce-scatter.11.cloned.1.call-start = ((), (), s32[]{:S(2)}) async-start(), calls=%async_computation.7 | async-start | bytes 2506752 | tf_op jit(solution)/shard_map/reduce_scatter | solution.py:89
  28.5 630.6 %reduce-scatter.7.cloned.1.call-start = ((), (), s32[]{:S(2)}) async-start(), calls=%async_computation.5 | async-start | bytes 2506752 | tf_op jit(solution)/shard_map/reduce_scatter | solution.py:77
  32.1 853.8 %reduce-scatter.9.cloned.1.call-start = ((), (), s32[]{:S(2)}) async-start(), calls=%async_computation.6 | async-start | bytes 2506752 | tf_op jit(solution)/shard_map/reduce_scatter | solution.py:83
  35.8 0.7 copy-start.7
  126.2 759.7 %copy-start.6 = (f32[384,2]{0,1:T(2,128)}, f32[384,2]{0,1:T(2,128)S(1)}, u32[]{:S(2)}) copy-start(f32[384,2]{0,1:T(2,128)S(1)} %constant_dynamic-update-slice_fusion) | copy-start | bytes 9220
  208.7 677.3 %copy-start.5 = (bf16[384,64]{0,1:T(8,128)(2,1)}, bf16[384,64]{0,1:T(8,128)(2,1)S(1)}, u32[]{:S(2)}) copy-start(bf16[384,64]{0,1:T(8,128)(2,1)S(1)} %slice_dynamic-update-slice_fusion) | copy-start | bytes 147460
Sparse Core Ops, SparseCore 0:
  24.6 183.1 reduce-scatter.4
  214.3 217.8 reduce-scatter.10
  438.7 220.4 reduce-scatter.6
  665.5 220.3 reduce-scatter.8
where the time goes:
time: 896 us; the launch traced here: 892 us
  waiting for transfers between devices  759 us (85%)
  blocking collectives  89.6 us (10%)
  matrix products  19.2 us (2%)
  between operations  15.9 us (2%)
    reduce_scatter x1, waiting for transfers between devices, body(): lax.psum_scatter(contract_lead(rows_in, d_pre_gate).astype(jnp.bfloat16),...  227 us
    reduce_scatter x1, waiting for transfers between devices, body(): lax.psum_scatter(contract_lead(rows_in, d_pre_up).astype(jnp.bfloat16), '...  227 us
    reduce_scatter x1, waiting for transfers between devices, body(): lax.psum_scatter(contract_lead(rows_cot, scaled_hidden).astype(jnp.bfloat...  224 us
    psum x1, blocking collectives, body(): dots = lax.psum(partial_dots, 'blk')  89.6 us
    reduce_scatter x1, waiting for transfers between devices, body(): lax.psum_scatter(input_terms, 'blk', scatter_dimension=1, tiled=True)  81.6 us
  transfers between devices with their start and end apart: 4, of which 4 were waited for; matrix products, arithmetic and copies ran while one was open for 1% of the time, Pallas kernels for 0%

commit v1 on v0

v1 whole, which is shorter than its diff:
```python
import jax
import jax.numpy as jnp
from jax import lax
from jax.experimental import pallas as pl
from jax.experimental.pallas import tpu as pltpu
from jax.sharding import PartitionSpec as P

MESH = pl.DeviceIdType.MESH
BF = jnp.bfloat16
F32 = jnp.float32

D = 3072
HID = 384
BLOCK = 128
TOK = 384
ROWS = 256
NY = 8
NZ = 12
SHARD = 192
FEAT = 64
CHUNK = 384

DOWN, UP = 0, 1
HOPS = {(0, DOWN): 4, (0, UP): 3, (1, DOWN): 3, (1, UP): 4, (2, DOWN): 4, (2, UP): 3, (3, DOWN): 3, (3, UP): 4}


def dot_lead(left, right):
    return lax.dot_general(left, right, (((0,), (0,)), ((), ())), preferred_element_type=F32)


def dot_last(left, right):
    return lax.dot_general(left, right, (((1,), (1,)), ((), ())), preferred_element_type=F32)


def kernel(
    list_ref, count_ref, probs_ref, slots_ref, tok_hbm, cot_hbm, wg_hbm, wu_hbm, wd_hbm,
    gtok_out, gprob_out, gg_out, gu_out, gd_out,
    tok, cot, wg, wu, wd, rin, rct, f_gate, f_up, f_back, hid, scaled, dpre, fac, picks,
    p_down, p_gu, x_recv, y_recv, ax_send, ax_recv,
    dx_send, dx_core, dx_z, dx_xl, dx_xlr, dt_send, dt_core, dt_z, dt_xl, dt_xlr,
    load_sem, xs_sem, xr_sem, ys_sem, yr_sem, as_sem, cs_sem, cr_sem, zs_sem, zr_sem,
):
    blk = lax.axis_index("blk")
    dp = lax.axis_index("dp")
    z = blk // 4
    xl = lax.rem(blk // 2, 2)
    core = lax.rem(blk, 2)
    y = dp // 2
    half = lax.rem(dp, 2)
    other = 1 - half

    def at(zz=None, xx=None, cc=None):
        zz = z if zz is None else zz
        xx = xl if xx is None else xx
        cc = core if cc is None else cc
        return (zz * 4 + xx * 2 + cc, dp)

    y_dev = {
        DOWN: (blk, lax.rem(y + NY - 1, NY) * 2 + half),
        UP: (blk, lax.rem(y + 1, NY) * 2 + half),
    }
    x_dev = (blk, y * 2 + other)
    core_dev = at(cc=1 - core)
    xl_dev = at(xx=1 - xl)

    def z_dev(step):
        return at(zz=lax.rem(z + step, NZ))

    loads = [
        pltpu.make_async_copy(src, dst, load_sem.at[i])
        for i, (src, dst) in enumerate(
            ((tok_hbm, tok), (wg_hbm, wg), (wu_hbm, wu), (cot_hbm, cot), (wd_hbm, wd))
        )
    ]
    for load in loads:
        load.start()

    barrier = pltpu.get_barrier_semaphore()
    for partner in (y_dev[DOWN], y_dev[UP], x_dev, core_dev, xl_dev):
        pl.semaphore_signal(barrier, inc=1, device_id=partner, device_id_type=MESH)
    for step in range(1, NZ):
        pl.semaphore_signal(barrier, inc=1, device_id=z_dev(step), device_id_type=MESH)

    blocks = [list_ref[0, k] for k in range(2)]
    live = [(count_ref[0] > k).astype(F32) for k in range(2)]
    is_block = [[(block == j).astype(F32) for j in range(3)] for block in blocks]

    gates_row = jnp.where(slots_ref[...] == 0, probs_ref[0:1, :], probs_ref[1:2, :])
    diagonal = lax.broadcasted_iota(jnp.int32, (BLOCK, BLOCK), 0) == lax.broadcasted_iota(
        jnp.int32, (BLOCK, BLOCK), 1
    )
    columns = [
        jnp.sum(jnp.where(diagonal, gates_row[:, j * BLOCK : (j + 1) * BLOCK], 0.0), axis=1, keepdims=True)
        for j in range(3)
    ]
    for k in range(2):
        column = sum(columns[j] * is_block[k][j] for j in range(3))
        fac[k * BLOCK : (k + 1) * BLOCK, :] = jnp.broadcast_to(column * live[k], (BLOCK, BLOCK))
        for j in range(3):
            picks[k, j] = jnp.broadcast_to(is_block[k][j], (16, 128)).astype(BF)

    def take_rows(source, target):
        def step(i, carry):
            for col in range(0, D, 128):
                parts = [source[pl.ds(pl.multiple_of(j * BLOCK + i * 16, 16), 16), col : col + 128] for j in range(3)]
                for k in range(2):
                    target[pl.ds(pl.multiple_of(k * BLOCK + i * 16, 16), 16), col : col + 128] = (
                        parts[0] * picks[k, 0] + parts[1] * picks[k, 1] + parts[2] * picks[k, 2]
                    )
            return carry

        lax.fori_loop(0, BLOCK // 16, step, 0)

    loads[0].wait()
    take_rows(tok, rin)
    loads[1].wait()
    f_gate[...] = jnp.dot(rin[...], wg[...], preferred_element_type=F32)
    loads[2].wait()
    f_up[...] = jnp.dot(rin[...], wu[...], preferred_element_type=F32)
    loads[3].wait()
    take_rows(cot, rct)

    def factor_rows(rows):
        column = fac[rows, :]
        return jnp.concatenate([column, column, column], axis=1)

    def first_part(i, carry):
        rows = pl.ds(pl.multiple_of(i * 32, 32), 32)
        pre_gate = f_gate[rows, :]
        pre_up = f_up[rows, :]
        sig = jax.nn.sigmoid(pre_gate)
        act = pre_gate * sig
        hidden = (act * pre_up).astype(BF)
        hid[rows, :] = hidden
        scaled[rows, :] = (hidden.astype(F32) * factor_rows(rows)).astype(BF)
        f_gate[rows, :] = pre_up * sig * (1.0 + pre_gate * (1.0 - sig))
        f_up[rows, :] = act
        return carry

    lax.fori_loop(0, ROWS // 32, first_part, 0)

    def dest(i):
        sign = 2 * (i % 2) - 1
        return lax.rem(y + 2 * NY + sign * (4 - (i + 1) // 2), NY)

    def order_of(direction, hop):
        if hop == 4:
            return 0
        return 7 - 2 * hop if direction == UP else 8 - 2 * hop

    def cols_of(t):
        return pl.ds(pl.multiple_of(t * CHUNK, CHUNK), CHUNK)

    def down_partial(i, carry):
        t = dest(i)
        part = dot_lead(rct[:, cols_of(t)], scaled[...]).astype(BF)
        p_down[t, 0] = part[:SHARD]
        p_down[t, 1] = part[SHARD:]
        return carry

    def y_copy(stream, direction, turn, src):
        return pltpu.make_async_remote_copy(
            src_ref=src,
            dst_ref=y_recv.at[stream, direction, turn],
            send_sem=ys_sem.at[stream, direction, turn],
            recv_sem=yr_sem.at[stream, direction, turn],
            device_id=y_dev[direction],
            device_id_type=MESH,
        )

    y_copies = {}

    def y_send(stream, direction, turn, src):
        copy = y_copy(stream, direction, turn, src)
        copy.start()
        y_copies[stream, direction, turn] = copy

    def own(stream, direction, hop):
        i = order_of(direction, hop)
        t = dest(i)
        if stream < 2:
            return p_down[t, other if stream == 0 else half].astype(F32)
        return p_gu[t, half, stream - 2].astype(F32) + x_recv[i, stream - 2].astype(F32)

    def first_turn_down(stream, direction):
        t = dest(order_of(direction, HOPS[stream, direction]))
        y_send(stream, direction, 0, p_down.at[t, other if stream == 0 else half])

    def forward_turn(stream, direction, turn):
        y_copies[stream, direction, turn - 1].wait_recv()
        slot = y_recv.at[stream, direction, turn - 1]
        slot[...] = (slot[...].astype(F32) + own(stream, direction, HOPS[stream, direction] - turn)).astype(BF)
        y_send(stream, direction, turn, slot)

    def last_sum(stream):
        total = own(stream, UP, 0)
        for direction in (DOWN, UP):
            turn = HOPS[stream, direction] - 1
            y_copies[stream, direction, turn].wait_recv()
            total = total + y_recv[stream, direction, turn].astype(F32)
        return total

    lax.fori_loop(0, 3, down_partial, 0)
    pl.semaphore_wait(barrier, 5 + NZ - 1)
    first_turn_down(0, DOWN)
    first_turn_down(1, UP)
    first_turn_down(0, UP)
    first_turn_down(1, DOWN)
    lax.fori_loop(3, NY, down_partial, 0)

    loads[4].wait()
    f_back[...] = jnp.dot(rct[...], wd[...], preferred_element_type=F32)

    def second_part(i, carry):
        rows = pl.ds(pl.multiple_of(i * 32, 32), 32)
        back = f_back[rows, :]
        d_hidden = back * factor_rows(rows)
        dpre[rows, 0:HID] = (d_hidden * f_gate[rows, :]).astype(BF)
        dpre[rows, HID : 2 * HID] = (d_hidden * f_up[rows, :]).astype(BF)
        f_back[rows, :] = hid[rows, :].astype(F32) * back
        return carry

    lax.fori_loop(0, ROWS // 32, second_part, 0)

    def x_copy(i):
        return pltpu.make_async_remote_copy(
            src_ref=p_gu.at[dest(i), other],
            dst_ref=x_recv.at[i],
            send_sem=xs_sem.at[i],
            recv_sem=xr_sem.at[i],
            device_id=x_dev,
            device_id_type=MESH,
        )

    def gu_partial(i, carry):
        t = dest(i)
        part = dot_lead(rin[:, cols_of(t)], dpre[...]).astype(BF)
        for h in range(2):
            for which in range(2):
                p_gu[t, h, which] = part[h * SHARD : (h + 1) * SHARD, which * HID : (which + 1) * HID]
        x_copy(i).start()
        return carry

    lax.fori_loop(0, NY, gu_partial, 0)

    for stream, direction in ((0, DOWN), (1, UP), (0, UP), (1, DOWN)):
        forward_turn(stream, direction, 1)

    def dx_part(q, carry):
        rows = pl.ds(pl.multiple_of(q * CHUNK, CHUNK), CHUNK)
        part = (dot_last(wg[rows, :], dpre[:, 0:HID]) + dot_last(wu[rows, :], dpre[:, HID : 2 * HID])).astype(BF)
        for m in range(6):
            dx_send[m % 2, 3 * q + m // 2] = part[m * FEAT : (m + 1) * FEAT]
        return carry

    lax.fori_loop(0, D // CHUNK, dx_part, 0)
    folded = f_back[:, 0:128] + f_back[:, 128:256] + f_back[:, 256:384]
    dots = jnp.sum(folded.T, axis=0, keepdims=True)
    dt_send[...] = jnp.broadcast_to(dots, (8, ROWS))

    def plain_copy(src, dst, send, recv, device):
        copy = pltpu.make_async_remote_copy(
            src_ref=src, dst_ref=dst, send_sem=send, recv_sem=recv, device_id=device, device_id_type=MESH
        )
        copy.start()
        return copy

    dx_core_copy = plain_copy(dx_send.at[1 - core], dx_core, cs_sem.at[0], cr_sem.at[0], core_dev)
    dt_core_copy = plain_copy(dt_send, dt_core, cs_sem.at[1], cr_sem.at[1], core_dev)

    def first_turn_gu(stream, direction):
        i = order_of(direction, HOPS[stream, direction])
        slot = x_recv.at[i, stream - 2]
        slot[...] = own(stream, direction, HOPS[stream, direction]).astype(BF)
        y_send(stream, direction, 0, slot)

    def x_arrived(i):
        x_copy(i).wait_recv()

    x_arrived(0)
    first_turn_gu(2, DOWN)
    first_turn_gu(3, UP)
    x_arrived(1)
    x_arrived(2)
    first_turn_gu(2, UP)
    first_turn_gu(3, DOWN)

    dx_core_copy.wait_recv()
    dt_core_copy.wait_recv()

    def add_core(i, carry):
        dx_core[i] = (dx_core[i].astype(F32) + dx_send[core, i].astype(F32)).astype(BF)
        return carry

    lax.fori_loop(0, 2 * NZ, add_core, 0)
    dt_z[0] = dt_send[...] + dt_core[...]

    def z_copy(step):
        target = lax.rem(z + step, NZ)
        return pltpu.make_async_remote_copy(
            src_ref=dx_core.at[pl.ds(2 * target, 2)],
            dst_ref=dx_z.at[step],
            send_sem=zs_sem.at[0, step],
            recv_sem=zr_sem.at[0, step],
            device_id=z_dev(step),
            device_id_type=MESH,
        )

    def z_dot_copy(step):
        return pltpu.make_async_remote_copy(
            src_ref=dt_z.at[0],
            dst_ref=dt_z.at[step],
            send_sem=zs_sem.at[1, step],
            recv_sem=zr_sem.at[1, step],
            device_id=z_dev(step),
            device_id_type=MESH,
        )

    def z_start(step, carry):
        z_copy(step).start()
        z_dot_copy(step).start()
        return carry

    lax.fori_loop(1, NZ, z_start, 0)

    for stream, direction in ((0, DOWN), (1, UP), (0, UP), (1, DOWN)):
        forward_turn(stream, direction, 2)
    x_arrived(3)
    x_arrived(4)
    for stream, direction in ((2, DOWN), (3, UP), (2, UP), (3, DOWN)):
        forward_turn(stream, direction, 1)
    forward_turn(0, DOWN, 3)
    forward_turn(1, UP, 3)

    def z_wait(step, carry):
        z_copy(step).wait_recv()
        z_dot_copy(step).wait_recv()
        return carry

    lax.fori_loop(1, NZ, z_wait, 0)

    def z_sum(step, total):
        return total + dx_z[step].astype(F32)

    dx_sum = lax.fori_loop(1, NZ, z_sum, dx_core[pl.ds(2 * z, 2)].astype(F32))
    dots = dt_z[z]
    for source in range(1, NZ):
        dots = dots + dt_z[lax.rem(z + NZ - source, NZ)]
    f_back[0:FEAT, 0:ROWS] = dx_sum[0]
    f_back[FEAT : 2 * FEAT, 0:ROWS] = dx_sum[1]
    dx_xl[...] = f_back[pl.ds(pl.multiple_of((1 - xl) * FEAT, FEAT), FEAT), 0:ROWS].astype(BF)
    dt_xl[...] = dots
    dx_xl_copy = plain_copy(dx_xl, dx_xlr, cs_sem.at[2], cr_sem.at[2], xl_dev)
    dt_xl_copy = plain_copy(dt_xl, dt_xlr, cs_sem.at[3], cr_sem.at[3], xl_dev)

    ax_send[...] = last_sum(0).astype(BF)
    ax_copy = plain_copy(ax_send, ax_recv, as_sem.at[0], as_sem.at[1], x_dev)

    x_arrived(5)
    x_arrived(6)
    for stream, direction in ((2, DOWN), (3, UP), (2, UP), (3, DOWN)):
        forward_turn(stream, direction, 2)

    dx_xl_copy.wait_recv()
    dt_xl_copy.wait_recv()
    grads = f_back[pl.ds(pl.multiple_of(xl * FEAT, FEAT), FEAT), 0:ROWS] + dx_xlr[...].astype(F32)
    dots = dt_xl[0:1, :] + dt_xlr[0:1, :]
    for j in range(3):
        block_cols = slice(j * BLOCK, (j + 1) * BLOCK)
        gtok_out[:, block_cols] = (
            grads[:, 0:BLOCK] * is_block[0][j] + grads[:, BLOCK:ROWS] * is_block[1][j]
        ).astype(BF)
        values = dots[:, 0:BLOCK] * (is_block[0][j] * live[0]) + dots[:, BLOCK:ROWS] * (is_block[1][j] * live[1])
        slots = slots_ref[:, block_cols]
        gprob_out[0:1, block_cols] = jnp.where(slots == 0, values, 0.0)
        gprob_out[1:2, block_cols] = jnp.where(slots == 1, values, 0.0)

    forward_turn(2, DOWN, 3)
    forward_turn(3, UP, 3)
    down_sum = last_sum(1)
    ax_copy.wait_recv()
    gd_out[...] = (down_sum + ax_recv[...].astype(F32)).astype(BF)
    x_arrived(7)
    gg_out[...] = last_sum(2).astype(BF)
    gu_out[...] = last_sum(3).astype(BF)

    for copy in y_copies.values():
        copy.wait_send()
    for copy in (dx_core_copy, dt_core_copy, dx_xl_copy, dt_xl_copy, ax_copy):
        copy.wait_send()

    def sent(i, carry):
        x_copy(i).wait_send()
        return carry

    lax.fori_loop(0, NY, sent, 0)

    def z_sent(step, carry):
        z_copy(step).wait_send()
        z_dot_copy(step).wait_send()
        return carry

    lax.fori_loop(1, NZ, z_sent, 0)


def body(tokens, cotangent, w_gate, w_up, w_down_t, gate_probs, slot_ids, block_list, block_count):
    smem = pl.BlockSpec(memory_space=pltpu.SMEM)
    vmem = pl.BlockSpec(memory_space=pltpu.VMEM)
    anywhere = pl.BlockSpec(memory_space=pl.ANY)
    dma = pltpu.SemaphoreType.DMA
    shard = (SHARD, HID)
    gtok, gprob, gg, gu, gd = pl.pallas_call(
        kernel,
        out_shape=(
            jax.ShapeDtypeStruct((FEAT, TOK), BF),
            jax.ShapeDtypeStruct((2, TOK), F32),
            jax.ShapeDtypeStruct(shard, BF),
            jax.ShapeDtypeStruct(shard, BF),
            jax.ShapeDtypeStruct(shard, BF),
        ),
        in_specs=[smem, smem, vmem, vmem] + [anywhere] * 5,
        out_specs=(vmem,) * 5,
        scratch_shapes=[
            pltpu.VMEM((TOK, D), BF),
            pltpu.VMEM((TOK, D), BF),
            pltpu.VMEM((D, HID), BF),
            pltpu.VMEM((D, HID), BF),
            pltpu.VMEM((D, HID), BF),
            pltpu.VMEM((ROWS, D), BF),
            pltpu.VMEM((ROWS, D), BF),
            pltpu.VMEM((ROWS, HID), F32),
            pltpu.VMEM((ROWS, HID), F32),
            pltpu.VMEM((ROWS, HID), F32),
            pltpu.VMEM((ROWS, HID), BF),
            pltpu.VMEM((ROWS, HID), BF),
            pltpu.VMEM((ROWS, 2 * HID), BF),
            pltpu.VMEM((ROWS, BLOCK), F32),
            pltpu.VMEM((2, 3, 16, 128), BF),
            pltpu.VMEM((NY, 2) + shard, BF),
            pltpu.VMEM((NY, 2, 2) + shard, BF),
            pltpu.VMEM((NY, 2) + shard, BF),
            pltpu.VMEM((4, 2, 4) + shard, BF),
            pltpu.VMEM(shard, BF),
            pltpu.VMEM(shard, BF),
            pltpu.VMEM((2, 2 * NZ, FEAT, ROWS), BF),
            pltpu.VMEM((2 * NZ, FEAT, ROWS), BF),
            pltpu.VMEM((NZ, 2, FEAT, ROWS), BF),
            pltpu.VMEM((FEAT, ROWS), BF),
            pltpu.VMEM((FEAT, ROWS), BF),
            pltpu.VMEM((8, ROWS), F32),
            pltpu.VMEM((8, ROWS), F32),
            pltpu.VMEM((NZ, 8, ROWS), F32),
            pltpu.VMEM((8, ROWS), F32),
            pltpu.VMEM((8, ROWS), F32),
            dma((5,)),
            dma((NY,)),
            dma((NY,)),
            dma((4, 2, 4)),
            dma((4, 2, 4)),
            dma((2,)),
            dma((4,)),
            dma((4,)),
            dma((2, NZ)),
            dma((2, NZ)),
        ],
        compiler_params=pltpu.CompilerParams(
            collective_id=0, has_side_effects=True, vmem_limit_bytes=52 * 1024 * 1024
        ),
        name="expert_backward",
    )(
        block_list, block_count, gate_probs.T, slot_ids.reshape(1, TOK),
        tokens, cotangent, w_gate, w_up, w_down_t,
    )
    return gtok.T, gprob.T, gg, gu, gd


def solution(mesh):
    placed = (
        P("dp", None),
        P("dp", None),
        P(None, "blk"),
        P(None, "blk"),
        P(None, "blk"),
        P("dp", None),
        P("dp"),
        P("dp", None),
        P("dp"),
    )
    return jax.shard_map(
        body,
        mesh=mesh,
        in_specs=placed,
        out_specs=(P("dp", "blk"), P("dp", None), P("dp", "blk"), P("dp", "blk"), P("dp", "blk")),
        check_vma=False,
    )
```

time: 896 us -> 94.1 us (0.11)
  the two profiles are of different devices: /device:TPU:1 before, /device:TPU:16 now
where the time goes in v1:
time: 94.1 us; the launch traced here: 93.9 us
  Pallas kernels  87.4 us (93%)
  local copies, waits for them, and re-layouts  5.2 us (6%)
  between operations  1.29 us (1%)
    pallas_call x1, Pallas kernels, body(): pl.pallas_call(kernel, out_shape=(jax.ShapeDtypeStruct((FEAT, TOK), BF),...  87.4 us
    unnamed x9, local copies, waits for them, and re-layouts  4.52 us

profile of v1, /device:TPU:16, one launch (start us, length us, event | category | flops | bytes accessed | tf_op | source)
XLA Modules:
  0.0 93.9 jit_solution(6136253280732537363)
XLA Ops:
  1.3 0.7 reshape.13.slots_ref
  2.0 0.0 copy-start
  2.0 0.7 copy-done
  2.6 0.0 copy-start.1
  2.6 0.7 copy-done.1
  3.3 87.4 %expert_backward.1 = (bf16[64,384]{1,0:T(8,128)(2,1)S(1)}, f32[2,384]{1,0:T(2,128)S(1)}, bf16[192,384]{1,0:T(8,128)(2,1)S(1)}, bf16[192,384]{1,0:T(8,128)(2,1)S(1)}, bf16[192,384]{1,0:T(8,128)(2,1)S(1)}) custom-call(s32[1,2]{1,0:T(1,128)S(1)} %copy-done.1, s32[1]{0:T(128)S(6)} %copy.19.count_ref, f32[2,384]{1,0:T(2,128)S(1)} %bitcast.4, ...), custom_call_target="tpu_custom_call" | custom-call | tf_op jit(solution)/shard_map/expert_backward/pallas_call | solution.py:412
  90.7 0.6 copy.20
  91.3 0.6 copy.21
  91.9 0.7 copy.22
  92.5 0.7 copy.23
  93.2 0.7 copy.24
Async XLA Ops:
  2.0 0.7 copy-start
  2.6 0.7 copy-start.1

commit v2 on v1

--- a/solution.py
+++ b/solution.py
@@ -35,8 +35,8 @@
 def kernel(
     list_ref, count_ref, probs_ref, slots_ref, tok_hbm, cot_hbm, wg_hbm, wu_hbm, wd_hbm,
     gtok_out, gprob_out, gg_out, gu_out, gd_out,
-    tok, cot, wg, wu, wd, rin, rct, f_gate, f_up, f_back, hid, scaled, dpre, fac, picks,
-    p_down, p_gu, x_recv, y_recv, ax_send, ax_recv,
+    tok, cot, wgu, wd, rin, rct, f_gu, f_back, hid, scaled, dpre, fac, picks,
+    rows_t, rows_x, dpre_x, p_down, p_gu, y_recv, ax_send, ax_recv,
     dx_send, dx_core, dx_z, dx_xl, dx_xlr, dt_send, dt_core, dt_z, dt_xl, dt_xlr,
     load_sem, xs_sem, xr_sem, ys_sem, yr_sem, as_sem, cs_sem, cr_sem, zs_sem, zr_sem,
 ):
@@ -69,7 +69,13 @@
     loads = [
         pltpu.make_async_copy(src, dst, load_sem.at[i])
         for i, (src, dst) in enumerate(
-            ((tok_hbm, tok), (wg_hbm, wg), (wu_hbm, wu), (cot_hbm, cot), (wd_hbm, wd))
+            (
+                (tok_hbm, tok),
+                (wg_hbm, wgu.at[:, 0:HID]),
+                (wu_hbm, wgu.at[:, HID : 2 * HID]),
+                (cot_hbm, cot),
+                (wd_hbm, wd),
+            )
         )
     ]
     for load in loads:
@@ -113,10 +119,31 @@
 
     loads[0].wait()
     take_rows(tok, rin)
+
+    def cols_of(t):
+        return pl.ds(pl.multiple_of(t * CHUNK, CHUNK), CHUNK)
+
+    def turn_rows(t, carry):
+        part = rin[:, cols_of(t)].T
+        rows_t[t, 0] = part[:SHARD]
+        rows_t[t, 1] = part[SHARD:]
+        return carry
+
+    lax.fori_loop(0, NY, turn_rows, 0)
+    pl.semaphore_wait(barrier, 5 + NZ - 1)
+
+    def plain_copy(src, dst, send, recv, device):
+        copy = pltpu.make_async_remote_copy(
+            src_ref=src, dst_ref=dst, send_sem=send, recv_sem=recv, device_id=device, device_id_type=MESH
+        )
+        copy.start()
+        return copy
+
+    rows_copy = plain_copy(rows_t.at[:, other], rows_x, xs_sem.at[0], xr_sem.at[0], x_dev)
+
     loads[1].wait()
-    f_gate[...] = jnp.dot(rin[...], wg[...], preferred_element_type=F32)
     loads[2].wait()
-    f_up[...] = jnp.dot(rin[...], wu[...], preferred_element_type=F32)
+    f_gu[...] = jnp.dot(rin[...], wgu[...], preferred_element_type=F32)
     loads[3].wait()
     take_rows(cot, rct)
 
@@ -126,15 +153,15 @@
 
     def first_part(i, carry):
         rows = pl.ds(pl.multiple_of(i * 32, 32), 32)
-        pre_gate = f_gate[rows, :]
-        pre_up = f_up[rows, :]
+        pre_gate = f_gu[rows, 0:HID]
+        pre_up = f_gu[rows, HID : 2 * HID]
         sig = jax.nn.sigmoid(pre_gate)
         act = pre_gate * sig
         hidden = (act * pre_up).astype(BF)
         hid[rows, :] = hidden
         scaled[rows, :] = (hidden.astype(F32) * factor_rows(rows)).astype(BF)
-        f_gate[rows, :] = pre_up * sig * (1.0 + pre_gate * (1.0 - sig))
-        f_up[rows, :] = act
+        f_gu[rows, 0:HID] = pre_up * sig * (1.0 + pre_gate * (1.0 - sig))
+        f_gu[rows, HID : 2 * HID] = act
         return carry
 
     lax.fori_loop(0, ROWS // 32, first_part, 0)
@@ -147,9 +174,6 @@
         if hop == 4:
             return 0
         return 7 - 2 * hop if direction == UP else 8 - 2 * hop
-
-    def cols_of(t):
-        return pl.ds(pl.multiple_of(t * CHUNK, CHUNK), CHUNK)
 
     def down_partial(i, carry):
         t = dest(i)
@@ -180,11 +204,14 @@
         t = dest(i)
         if stream < 2:
             return p_down[t, other if stream == 0 else half].astype(F32)
-        return p_gu[t, half, stream - 2].astype(F32) + x_recv[i, stream - 2].astype(F32)
-
-    def first_turn_down(stream, direction):
+        return p_gu[t, stream - 2].astype(F32)
+
+    def first_turn(stream, direction):
         t = dest(order_of(direction, HOPS[stream, direction]))
-        y_send(stream, direction, 0, p_down.at[t, other if stream == 0 else half])
+        if stream < 2:
+            y_send(stream, direction, 0, p_down.at[t, other if stream == 0 else half])
+        else:
+            y_send(stream, direction, 0, p_gu.at[t, stream - 2])
 
     def forward_turn(stream, direction, turn):
         y_copies[stream, direction, turn - 1].wait_recv()
@@ -201,11 +228,8 @@
         return total
 
     lax.fori_loop(0, 3, down_partial, 0)
-    pl.semaphore_wait(barrier, 5 + NZ - 1)
-    first_turn_down(0, DOWN)
-    first_turn_down(1, UP)
-    first_turn_down(0, UP)
-    first_turn_down(1, DOWN)
+    for stream, direction in ((0, DOWN), (1, UP), (0, UP), (1, DOWN)):
+        first_turn(stream, direction)
     lax.fori_loop(3, NY, down_partial, 0)
 
     loads[4].wait()
@@ -215,40 +239,31 @@
         rows = pl.ds(pl.multiple_of(i * 32, 32), 32)
         back = f_back[rows, :]
         d_hidden = back * factor_rows(rows)
-        dpre[rows, 0:HID] = (d_hidden * f_gate[rows, :]).astype(BF)
-        dpre[rows, HID : 2 * HID] = (d_hidden * f_up[rows, :]).astype(BF)
+        dpre[rows, 0:HID] = (d_hidden * f_gu[rows, 0:HID]).astype(BF)
+        dpre[rows, HID : 2 * HID] = (d_hidden * f_gu[rows, HID : 2 * HID]).astype(BF)
         f_back[rows, :] = hid[rows, :].astype(F32) * back
         return carry
 
     lax.fori_loop(0, ROWS // 32, second_part, 0)
 
-    def x_copy(i):
-        return pltpu.make_async_remote_copy(
-            src_ref=p_gu.at[dest(i), other],
-            dst_ref=x_recv.at[i],
-            send_sem=xs_sem.at[i],
-            recv_sem=xr_sem.at[i],
-            device_id=x_dev,
-            device_id_type=MESH,
-        )
+    dpre_copy = plain_copy(dpre, dpre_x, xs_sem.at[1], xr_sem.at[1], x_dev)
 
     def gu_partial(i, carry):
         t = dest(i)
-        part = dot_lead(rin[:, cols_of(t)], dpre[...]).astype(BF)
-        for h in range(2):
-            for which in range(2):
-                p_gu[t, h, which] = part[h * SHARD : (h + 1) * SHARD, which * HID : (which + 1) * HID]
-        x_copy(i).start()
-        return carry
-
-    lax.fori_loop(0, NY, gu_partial, 0)
+        part = (
+            jnp.dot(rows_t[t, half], dpre[...], preferred_element_type=F32)
+            + jnp.dot(rows_x[t], dpre_x[...], preferred_element_type=F32)
+        ).astype(BF)
+        p_gu[t, 0] = part[:, 0:HID]
+        p_gu[t, 1] = part[:, HID : 2 * HID]
+        return carry
 
     for stream, direction in ((0, DOWN), (1, UP), (0, UP), (1, DOWN)):
         forward_turn(stream, direction, 1)
 
     def dx_part(q, carry):
         rows = pl.ds(pl.multiple_of(q * CHUNK, CHUNK), CHUNK)
-        part = (dot_last(wg[rows, :], dpre[:, 0:HID]) + dot_last(wu[rows, :], dpre[:, HID : 2 * HID])).astype(BF)
+        part = dot_last(wgu[rows, :], dpre[...]).astype(BF)
         for m in range(6):
             dx_send[m % 2, 3 * q + m // 2] = part[m * FEAT : (m + 1) * FEAT]
         return carry
@@ -258,32 +273,18 @@
     dots = jnp.sum(folded.T, axis=0, keepdims=True)
     dt_send[...] = jnp.broadcast_to(dots, (8, ROWS))
 
-    def plain_copy(src, dst, send, recv, device):
-        copy = pltpu.make_async_remote_copy(
-            src_ref=src, dst_ref=dst, send_sem=send, recv_sem=recv, device_id=device, device_id_type=MESH
-        )
-        copy.start()
-        return copy
-
     dx_core_copy = plain_copy(dx_send.at[1 - core], dx_core, cs_sem.at[0], cr_sem.at[0], core_dev)
     dt_core_copy = plain_copy(dt_send, dt_core, cs_sem.at[1], cr_sem.at[1], core_dev)
 
-    def first_turn_gu(stream, direction):
-        i = order_of(direction, HOPS[stream, direction])
-        slot = x_recv.at[i, stream - 2]
-        slot[...] = own(stream, direction, HOPS[stream, direction]).astype(BF)
-        y_send(stream, direction, 0, slot)
-
-    def x_arrived(i):
-        x_copy(i).wait_recv()
-
-    x_arrived(0)
-    first_turn_gu(2, DOWN)
-    first_turn_gu(3, UP)
-    x_arrived(1)
-    x_arrived(2)
-    first_turn_gu(2, UP)
-    first_turn_gu(3, DOWN)
+    for stream, direction in ((0, DOWN), (1, UP), (0, UP), (1, DOWN)):
+        forward_turn(stream, direction, 2)
+
+    rows_copy.wait_recv()
+    dpre_copy.wait_recv()
+    lax.fori_loop(0, 3, gu_partial, 0)
+    for stream, direction in ((2, DOWN), (3, UP), (2, UP), (3, DOWN)):
+        first_turn(stream, direction)
+    lax.fori_loop(3, NY, gu_partial, 0)
 
     dx_core_copy.wait_recv()
     dt_core_copy.wait_recv()
@@ -323,14 +324,10 @@
 
     lax.fori_loop(1, NZ, z_start, 0)
 
-    for stream, direction in ((0, DOWN), (1, UP), (0, UP), (1, DOWN)):
-        forward_turn(stream, direction, 2)
-    x_arrived(3)
-    x_arrived(4)
+    forward_turn(0, DOWN, 3)
+    forward_turn(1, UP, 3)
     for stream, direction in ((2, DOWN), (3, UP), (2, UP), (3, DOWN)):
         forward_turn(stream, direction, 1)
-    forward_turn(0, DOWN, 3)
-    forward_turn(1, UP, 3)
 
     def z_wait(step, carry):
         z_copy(step).wait_recv()
@@ -356,8 +353,6 @@
     ax_send[...] = last_sum(0).astype(BF)
     ax_copy = plain_copy(ax_send, ax_recv, as_sem.at[0], as_sem.at[1], x_dev)
 
-    x_arrived(5)
-    x_arrived(6)
     for stream, direction in ((2, DOWN), (3, UP), (2, UP), (3, DOWN)):
         forward_turn(stream, direction, 2)
 
@@ -380,20 +375,13 @@
     down_sum = last_sum(1)
     ax_copy.wait_recv()
     gd_out[...] = (down_sum + ax_recv[...].astype(F32)).astype(BF)
-    x_arrived(7)
     gg_out[...] = last_sum(2).astype(BF)
     gu_out[...] = last_sum(3).astype(BF)
 
     for copy in y_copies.values():
         copy.wait_send()
-    for copy in (dx_core_copy, dt_core_copy, dx_xl_copy, dt_xl_copy, ax_copy):
+    for copy in (rows_copy, dpre_copy, dx_core_copy, dt_core_copy, dx_xl_copy, dt_xl_copy, ax_copy):
         copy.wait_send()
-
-    def sent(i, carry):
-        x_copy(i).wait_send()
-        return carry
-
-    lax.fori_loop(0, NY, sent, 0)
 
     def z_sent(step, carry):
         z_copy(step).wait_send()
@@ -423,21 +411,21 @@
         scratch_shapes=[
             pltpu.VMEM((TOK, D), BF),
             pltpu.VMEM((TOK, D), BF),
-            pltpu.VMEM((D, HID), BF),
-            pltpu.VMEM((D, HID), BF),
+            pltpu.VMEM((D, 2 * HID), BF),
             pltpu.VMEM((D, HID), BF),
             pltpu.VMEM((ROWS, D), BF),
             pltpu.VMEM((ROWS, D), BF),
-            pltpu.VMEM((ROWS, HID), F32),
-            pltpu.VMEM((ROWS, HID), F32),
+            pltpu.VMEM((ROWS, 2 * HID), F32),
             pltpu.VMEM((ROWS, HID), F32),
             pltpu.VMEM((ROWS, HID), BF),
             pltpu.VMEM((ROWS, HID), BF),
             pltpu.VMEM((ROWS, 2 * HID), BF),
             pltpu.VMEM((ROWS, BLOCK), F32),
             pltpu.VMEM((2, 3, 16, 128), BF),
+            pltpu.VMEM((NY, 2, SHARD, ROWS), BF),
+            pltpu.VMEM((NY, SHARD, ROWS), BF),
+            pltpu.VMEM((ROWS, 2 * HID), BF),
             pltpu.VMEM((NY, 2) + shard, BF),
-            pltpu.VMEM((NY, 2, 2) + shard, BF),
             pltpu.VMEM((NY, 2) + shard, BF),
             pltpu.VMEM((4, 2, 4) + shard, BF),
             pltpu.VMEM(shard, BF),
@@ -453,8 +441,8 @@
             pltpu.VMEM((8, ROWS), F32),
             pltpu.VMEM((8, ROWS), F32),
             dma((5,)),
-            dma((NY,)),
-            dma((NY,)),
+            dma((2,)),
+            dma((2,)),
             dma((4, 2, 4)),
             dma((4, 2, 4)),
             dma((2,)),

time: 94.1 us -> 98.4 us (1.046)
  the two profiles are of different devices: /device:TPU:16 before, /device:TPU:1 now
where the time goes in v2:
time: 98.4 us; the launch traced here: 98.2 us
  Pallas kernels  91.7 us (93%)
  local copies, waits for them, and re-layouts  5.2 us (5%)
  between operations  1.29 us (1%)
    pallas_call x1, Pallas kernels, body(): pl.pallas_call(kernel, out_shape=(jax.ShapeDtypeStruct((FEAT, TOK), BF),...  91.7 us
    unnamed x9, local copies, waits for them, and re-layouts  4.52 us

profile of v2, /device:TPU:1, one launch (start us, length us, event | category | flops | bytes accessed | tf_op | source)
XLA Modules:
  0.0 98.2 jit_solution(13794387690515042777)
XLA Ops:
  1.3 0.7 reshape.13.slots_ref
  2.0 0.0 copy-start
  2.0 0.7 copy-done
  2.6 0.0 copy-start.1
  2.6 0.7 copy-done.1
  3.3 91.7 %expert_backward.1 = (bf16[64,384]{1,0:T(8,128)(2,1)S(1)}, f32[2,384]{1,0:T(2,128)S(1)}, bf16[192,384]{1,0:T(8,128)(2,1)S(1)}, bf16[192,384]{1,0:T(8,128)(2,1)S(1)}, bf16[192,384]{1,0:T(8,128)(2,1)S(1)}) custom-call(s32[1,2]{1,0:T(1,128)S(1)} %copy-done.1, s32[1]{0:T(128)S(6)} %copy.19.count_ref, f32[2,384]{1,0:T(2,128)S(1)} %bitcast.4, ...), custom_call_target="tpu_custom_call" | custom-call | tf_op jit(solution)/shard_map/expert_backward/pallas_call | solution.py:400
  95.0 0.6 copy.20
  95.6 0.6 copy.21
  96.2 0.7 copy.22
  96.9 0.7 copy.23
  97.5 0.7 copy.24
Async XLA Ops:
  2.0 0.7 copy-start
  2.6 0.7 copy-start.1

commit v3 on v2

--- a/solution.py
+++ b/solution.py
@@ -37,8 +37,8 @@
     gtok_out, gprob_out, gg_out, gu_out, gd_out,
     tok, cot, wgu, wd, rin, rct, f_gu, f_back, hid, scaled, dpre, fac, picks,
     rows_t, rows_x, dpre_x, p_down, p_gu, y_recv, ax_send, ax_recv,
-    dx_send, dx_core, dx_z, dx_xl, dx_xlr, dt_send, dt_core, dt_z, dt_xl, dt_xlr,
-    load_sem, xs_sem, xr_sem, ys_sem, yr_sem, as_sem, cs_sem, cr_sem, zs_sem, zr_sem,
+    dx_own, dx_core, dx_xl, dx_z, dx_out, dx_fin, dt_own, dt_core, dt_sum, dt_xl, dt_z, dt_out, dt_fin,
+    load_sem, xs_sem, xr_sem, ys_sem, yr_sem, as_sem, cs_sem, cr_sem, zs_sem, zr_sem, ready,
 ):
     blk = lax.axis_index("blk")
     dp = lax.axis_index("dp")
@@ -48,6 +48,7 @@
     y = dp // 2
     half = lax.rem(dp, 2)
     other = 1 - half
+    colour = lax.rem(y + half + xl + core, 2)
 
     def at(zz=None, xx=None, cc=None):
         zz = z if zz is None else zz
@@ -81,11 +82,15 @@
     for load in loads:
         load.start()
 
+    plane = (y_dev[DOWN], y_dev[UP], x_dev, core_dev, xl_dev)
     barrier = pltpu.get_barrier_semaphore()
-    for partner in (y_dev[DOWN], y_dev[UP], x_dev, core_dev, xl_dev):
-        pl.semaphore_signal(barrier, inc=1, device_id=partner, device_id_type=MESH)
-    for step in range(1, NZ):
-        pl.semaphore_signal(barrier, inc=1, device_id=z_dev(step), device_id_type=MESH)
+
+    @pl.when(colour == 0)
+    def _():
+        for partner in plane:
+            pl.semaphore_signal(barrier, inc=1, device_id=partner, device_id_type=MESH)
+        for step in range(1, NZ):
+            pl.semaphore_signal(barrier, inc=1, device_id=z_dev(step), device_id_type=MESH)
 
     blocks = [list_ref[0, k] for k in range(2)]
     live = [(count_ref[0] > k).astype(F32) for k in range(2)]
@@ -120,6 +125,12 @@
     loads[0].wait()
     take_rows(tok, rin)
 
+    @pl.when(colour == 1)
+    def _():
+        pl.semaphore_wait(barrier, len(plane))
+        for partner in plane:
+            pl.semaphore_signal(ready, inc=1, device_id=partner, device_id_type=MESH)
+
     def cols_of(t):
         return pl.ds(pl.multiple_of(t * CHUNK, CHUNK), CHUNK)
 
@@ -130,7 +141,11 @@
         return carry
 
     lax.fori_loop(0, NY, turn_rows, 0)
-    pl.semaphore_wait(barrier, 5 + NZ - 1)
+
+    @pl.when(colour == 0)
+    def _():
+        pl.semaphore_wait(ready, len(plane))
+
 
     def plain_copy(src, dst, send, recv, device):
         copy = pltpu.make_async_remote_copy(
@@ -139,7 +154,8 @@
         copy.start()
         return copy
 
-    rows_copy = plain_copy(rows_t.at[:, other], rows_x, xs_sem.at[0], xr_sem.at[0], x_dev)
+    mine = pl.ds((NY // 2) * core, NY // 2)
+    rows_copy = plain_copy(rows_t.at[mine, other], rows_x.at[mine], xs_sem.at[0], xr_sem.at[0], x_dev)
 
     loads[1].wait()
     loads[2].wait()
@@ -258,108 +274,151 @@
         p_gu[t, 1] = part[:, HID : 2 * HID]
         return carry
 
+    def dx_part(q, carry):
+        rows = pl.ds(pl.multiple_of(q * 8 * FEAT, 8 * FEAT), 8 * FEAT)
+        part = dot_last(wgu[rows, :], dpre[...]).astype(BF)
+        for m in range(8):
+            dx_own[(m // 2) % 2, 4 * q + 2 * (m // 4) + m % 2] = part[m * FEAT : (m + 1) * FEAT]
+        return carry
+
+    lax.fori_loop(0, D // (8 * FEAT), dx_part, 0)
+    folded = f_back[:, 0:128] + f_back[:, 128:256] + f_back[:, 256:384]
+    dots = jnp.sum(folded.T, axis=0, keepdims=True)
+    dt_own[...] = jnp.broadcast_to(dots, (8, ROWS))
+
+    dx_core_copy = plain_copy(dx_own.at[lax.rem(xl + 1 + colour, 2)], dx_core, cs_sem.at[0], cr_sem.at[0], core_dev)
+    dt_core_copy = plain_copy(dt_own, dt_core, cs_sem.at[1], cr_sem.at[1], core_dev)
+
+    rows_copy.wait_recv()
+    theirs = rows_x.at[mine]
+    pass_copy = plain_copy(theirs, theirs, xs_sem.at[2], xr_sem.at[2], core_dev)
+
     for stream, direction in ((0, DOWN), (1, UP), (0, UP), (1, DOWN)):
         forward_turn(stream, direction, 1)
 
-    def dx_part(q, carry):
-        rows = pl.ds(pl.multiple_of(q * CHUNK, CHUNK), CHUNK)
-        part = dot_last(wgu[rows, :], dpre[...]).astype(BF)
-        for m in range(6):
-            dx_send[m % 2, 3 * q + m // 2] = part[m * FEAT : (m + 1) * FEAT]
-        return carry
-
-    lax.fori_loop(0, D // CHUNK, dx_part, 0)
-    folded = f_back[:, 0:128] + f_back[:, 128:256] + f_back[:, 256:384]
-    dots = jnp.sum(folded.T, axis=0, keepdims=True)
-    dt_send[...] = jnp.broadcast_to(dots, (8, ROWS))
-
-    dx_core_copy = plain_copy(dx_send.at[1 - core], dx_core, cs_sem.at[0], cr_sem.at[0], core_dev)
-    dt_core_copy = plain_copy(dt_send, dt_core, cs_sem.at[1], cr_sem.at[1], core_dev)
-
-    for stream, direction in ((0, DOWN), (1, UP), (0, UP), (1, DOWN)):
-        forward_turn(stream, direction, 2)
-
-    rows_copy.wait_recv()
+    def remote(src, dst, send, recv, device):
+        return pltpu.make_async_remote_copy(
+            src_ref=src, dst_ref=dst, send_sem=send, recv_sem=recv, device_id=device, device_id_type=MESH
+        )
+
+    def dx_xl_copy():
+        return remote(dx_core, dx_xl, cs_sem.at[2], cr_sem.at[2], xl_dev)
+
+    def dt_xl_copy():
+        return remote(dt_sum, dt_xl, cs_sem.at[3], cr_sem.at[3], xl_dev)
+
+    def z_copy(step):
+        target = lax.rem(z + step, NZ)
+        return remote(
+            dx_core.at[pl.ds(2 * target, 2)], dx_z.at[step], zs_sem.at[0, step], zr_sem.at[0, step], z_dev(step)
+        )
+
+    def z_dot_copy(step):
+        return remote(dt_z.at[0], dt_z.at[step], zs_sem.at[1, step], zr_sem.at[1, step], z_dev(step))
+
+    def dx_out_copy():
+        return remote(dx_out, dx_fin, cs_sem.at[4], cr_sem.at[4], core_dev)
+
+    def dt_out_copy():
+        return remote(dt_fin, dt_out, cs_sem.at[5], cr_sem.at[5], core_dev)
+
+    dx_core_copy.wait_recv()
+    dt_core_copy.wait_recv()
+    dt_sum[...] = dt_own[...] + dt_core[...]
+
+    @pl.when(colour == 1)
+    def _():
+        def add_core(i, carry):
+            dx_core[i] = (dx_core[i].astype(F32) + dx_own[1 - xl, i].astype(F32)).astype(BF)
+            return carry
+
+        lax.fori_loop(0, 2 * NZ, add_core, 0)
+        dx_xl_copy().start()
+        dt_xl_copy().start()
+
     dpre_copy.wait_recv()
+    pass_copy.wait_recv()
     lax.fori_loop(0, 3, gu_partial, 0)
     for stream, direction in ((2, DOWN), (3, UP), (2, UP), (3, DOWN)):
         first_turn(stream, direction)
     lax.fori_loop(3, NY, gu_partial, 0)
 
-    dx_core_copy.wait_recv()
-    dt_core_copy.wait_recv()
-
-    def add_core(i, carry):
-        dx_core[i] = (dx_core[i].astype(F32) + dx_send[core, i].astype(F32)).astype(BF)
-        return carry
-
-    lax.fori_loop(0, 2 * NZ, add_core, 0)
-    dt_z[0] = dt_send[...] + dt_core[...]
-
-    def z_copy(step):
-        target = lax.rem(z + step, NZ)
-        return pltpu.make_async_remote_copy(
-            src_ref=dx_core.at[pl.ds(2 * target, 2)],
-            dst_ref=dx_z.at[step],
-            send_sem=zs_sem.at[0, step],
-            recv_sem=zr_sem.at[0, step],
-            device_id=z_dev(step),
-            device_id_type=MESH,
-        )
-
-    def z_dot_copy(step):
-        return pltpu.make_async_remote_copy(
-            src_ref=dt_z.at[0],
-            dst_ref=dt_z.at[step],
-            send_sem=zs_sem.at[1, step],
-            recv_sem=zr_sem.at[1, step],
-            device_id=z_dev(step),
-            device_id_type=MESH,
-        )
-
-    def z_start(step, carry):
-        z_copy(step).start()
-        z_dot_copy(step).start()
-        return carry
-
-    lax.fori_loop(1, NZ, z_start, 0)
+    for stream, direction in ((0, DOWN), (1, UP), (0, UP), (1, DOWN)):
+        forward_turn(stream, direction, 2)
+
+    @pl.when(colour == 0)
+    def _():
+        dx_xl_copy().wait_recv()
+        dt_xl_copy().wait_recv()
+
+        def add_four(i, carry):
+            dx_core[i] = (
+                dx_core[i].astype(F32) + dx_own[xl, i].astype(F32) + dx_xl[i].astype(F32)
+            ).astype(BF)
+            return carry
+
+        lax.fori_loop(0, 2 * NZ, add_four, 0)
+        dt_z[0] = dt_sum[...] + dt_xl[...]
+        pl.semaphore_wait(barrier, NZ - 1)
+
+        def z_start(step, carry):
+            z_copy(step).start()
+            z_dot_copy(step).start()
+            return carry
+
+        lax.fori_loop(1, NZ, z_start, 0)
 
     forward_turn(0, DOWN, 3)
     forward_turn(1, UP, 3)
     for stream, direction in ((2, DOWN), (3, UP), (2, UP), (3, DOWN)):
         forward_turn(stream, direction, 1)
 
-    def z_wait(step, carry):
-        z_copy(step).wait_recv()
-        z_dot_copy(step).wait_recv()
-        return carry
-
-    lax.fori_loop(1, NZ, z_wait, 0)
-
-    def z_sum(step, total):
-        return total + dx_z[step].astype(F32)
-
-    dx_sum = lax.fori_loop(1, NZ, z_sum, dx_core[pl.ds(2 * z, 2)].astype(F32))
-    dots = dt_z[z]
-    for source in range(1, NZ):
-        dots = dots + dt_z[lax.rem(z + NZ - source, NZ)]
-    f_back[0:FEAT, 0:ROWS] = dx_sum[0]
-    f_back[FEAT : 2 * FEAT, 0:ROWS] = dx_sum[1]
-    dx_xl[...] = f_back[pl.ds(pl.multiple_of((1 - xl) * FEAT, FEAT), FEAT), 0:ROWS].astype(BF)
-    dt_xl[...] = dots
-    dx_xl_copy = plain_copy(dx_xl, dx_xlr, cs_sem.at[2], cr_sem.at[2], xl_dev)
-    dt_xl_copy = plain_copy(dt_xl, dt_xlr, cs_sem.at[3], cr_sem.at[3], xl_dev)
-
     ax_send[...] = last_sum(0).astype(BF)
     ax_copy = plain_copy(ax_send, ax_recv, as_sem.at[0], as_sem.at[1], x_dev)
 
     for stream, direction in ((2, DOWN), (3, UP), (2, UP), (3, DOWN)):
         forward_turn(stream, direction, 2)
 
-    dx_xl_copy.wait_recv()
-    dt_xl_copy.wait_recv()
-    grads = f_back[pl.ds(pl.multiple_of(xl * FEAT, FEAT), FEAT), 0:ROWS] + dx_xlr[...].astype(F32)
-    dots = dt_xl[0:1, :] + dt_xlr[0:1, :]
+    forward_turn(2, DOWN, 3)
+    forward_turn(3, UP, 3)
+    @pl.when(colour == 0)
+    def _():
+        def z_wait(step, carry):
+            z_copy(step).wait_recv()
+            z_dot_copy(step).wait_recv()
+            return carry
+
+        lax.fori_loop(1, NZ, z_wait, 0)
+
+        def z_sum(step, total):
+            return total + dx_z[step].astype(F32)
+
+        dx_sum = lax.fori_loop(1, NZ, z_sum, dx_core[pl.ds(2 * z, 2)].astype(F32))
+        f_back[0:FEAT, 0:ROWS] = dx_sum[0]
+        f_back[FEAT : 2 * FEAT, 0:ROWS] = dx_sum[1]
+        dx_out[...] = f_back[pl.ds(pl.multiple_of((1 - core) * FEAT, FEAT), FEAT), 0:ROWS].astype(BF)
+        dx_fin[...] = f_back[pl.ds(pl.multiple_of(core * FEAT, FEAT), FEAT), 0:ROWS].astype(BF)
+        dots = dt_z[z]
+        for source in range(1, NZ):
+            dots = dots + dt_z[lax.rem(z + NZ - source, NZ)]
+        dt_fin[...] = dots
+        dt_out[...] = dots
+        dx_out_copy().start()
+        dt_out_copy().start()
+
+    down_sum = last_sum(1)
+    ax_copy.wait_recv()
+    gd_out[...] = (down_sum + ax_recv[...].astype(F32)).astype(BF)
+    gg_out[...] = last_sum(2).astype(BF)
+    gu_out[...] = last_sum(3).astype(BF)
+
+    @pl.when(colour == 1)
+    def _():
+        dx_out_copy().wait_recv()
+        dt_out_copy().wait_recv()
+
+    grads = dx_fin[...].astype(F32)
+    dots = dt_out[0:1, :]
     for j in range(3):
         block_cols = slice(j * BLOCK, (j + 1) * BLOCK)
         gtok_out[:, block_cols] = (
@@ -370,25 +429,36 @@
         gprob_out[0:1, block_cols] = jnp.where(slots == 0, values, 0.0)
         gprob_out[1:2, block_cols] = jnp.where(slots == 1, values, 0.0)
 
-    forward_turn(2, DOWN, 3)
-    forward_turn(3, UP, 3)
-    down_sum = last_sum(1)
-    ax_copy.wait_recv()
-    gd_out[...] = (down_sum + ax_recv[...].astype(F32)).astype(BF)
-    gg_out[...] = last_sum(2).astype(BF)
-    gu_out[...] = last_sum(3).astype(BF)
-
     for copy in y_copies.values():
         copy.wait_send()
-    for copy in (rows_copy, dpre_copy, dx_core_copy, dt_core_copy, dx_xl_copy, dt_xl_copy, ax_copy):
+    for copy in (rows_copy, pass_copy, dpre_copy, dx_core_copy, dt_core_copy, ax_copy):
         copy.wait_send()
 
-    def z_sent(step, carry):
-        z_copy(step).wait_send()
-        z_dot_copy(step).wait_send()
-        return carry
-
-    lax.fori_loop(1, NZ, z_sent, 0)
+    @pl.when(colour == 1)
+    def _():
+        dx_xl_copy().wait_send()
+        dt_xl_copy().wait_send()
+
+    @pl.when(colour == 0)
+    def _():
+        def z_sent(step, carry):
+            z_copy(step).wait_send()
+            z_dot_copy(step).wait_send()
+            return carry
+
+        lax.fori_loop(1, NZ, z_sent, 0)
+        dx_out_copy().wait_send()
+        dt_out_copy().wait_send()
+
+
+def finish(*refs):
+    sem = refs[-1]
+    count = len(refs) // 2
+    copies = [pltpu.make_async_copy(refs[i], refs[count + i], sem.at[i]) for i in range(count)]
+    for copy in copies:
+        copy.start()
+    for copy in copies:
+        copy.wait()
 
 
 def body(tokens, cotangent, w_gate, w_up, w_down_t, gate_probs, slot_ids, block_list, block_count):
@@ -397,7 +467,7 @@
     anywhere = pl.BlockSpec(memory_space=pl.ANY)
     dma = pltpu.SemaphoreType.DMA
     shard = (SHARD, HID)
-    gtok, gprob, gg, gu, gd = pl.pallas_call(
+    partial = pl.pallas_call(
         kernel,
         out_shape=(
             jax.ShapeDtypeStruct((FEAT, TOK), BF),
@@ -432,24 +502,28 @@
             pltpu.VMEM(shard, BF),
             pltpu.VMEM((2, 2 * NZ, FEAT, ROWS), BF),
             pltpu.VMEM((2 * NZ, FEAT, ROWS), BF),
+            pltpu.VMEM((2 * NZ, FEAT, ROWS), BF),
             pltpu.VMEM((NZ, 2, FEAT, ROWS), BF),
             pltpu.VMEM((FEAT, ROWS), BF),
             pltpu.VMEM((FEAT, ROWS), BF),
+            pltpu.VMEM((8, ROWS), F32),
+            pltpu.VMEM((8, ROWS), F32),
             pltpu.VMEM((8, ROWS), F32),
             pltpu.VMEM((8, ROWS), F32),
             pltpu.VMEM((NZ, 8, ROWS), F32),
             pltpu.VMEM((8, ROWS), F32),
             pltpu.VMEM((8, ROWS), F32),
             dma((5,)),
-            dma((2,)),
-            dma((2,)),
+            dma((3,)),
+            dma((3,)),
             dma((4, 2, 4)),
             dma((4, 2, 4)),
             dma((2,)),
-            dma((4,)),
-            dma((4,)),
+            dma((6,)),
+            dma((6,)),
             dma((2, NZ)),
             dma((2, NZ)),
+            pltpu.SemaphoreType.REGULAR,
         ],
         compiler_params=pltpu.CompilerParams(
             collective_id=0, has_side_effects=True, vmem_limit_bytes=52 * 1024 * 1024
@@ -459,6 +533,14 @@
         block_list, block_count, gate_probs.T, slot_ids.reshape(1, TOK),
         tokens, cotangent, w_gate, w_up, w_down_t,
     )
+    gtok, gprob, gg, gu, gd = pl.pallas_call(
+        finish,
+        out_shape=tuple(jax.ShapeDtypeStruct(part.shape, part.dtype) for part in partial),
+        in_specs=[anywhere] * 5,
+        out_specs=(anywhere,) * 5,
+        scratch_shapes=[dma((5,))],
+        name="finish",
+    )(*partial)
     return gtok.T, gprob.T, gg, gu, gd
 
 

time: 98.4 us -> 90.7 us (0.922)
  Pallas kernels: 91.7 us -> 84 us
    pallas_call x1, Pallas kernels: 91.7 us -> 67.9 us  [body(): pl.pallas_call(kernel, out_shape=(jax.ShapeDtypeStruct((FEAT, TOK), BF),...]
    pallas_call x0 -> x1, Pallas kernels: none -> 16.1 us  [body(): pl.pallas_call(finish, out_shape=tuple((jax.ShapeDtypeStruct(part.shape,...]
    unnamed x9 -> x14, local copies, waits for them, and re-layouts: 4.52 us -> 4.51 us
where the time goes in v3:
time: 90.7 us; the launch traced here: 90.5 us
  Pallas kernels  84 us (93%)
  local copies, waits for them, and re-layouts  5.19 us (6%)
  between operations  1.3 us (1%)
    pallas_call x1, Pallas kernels, body(): pl.pallas_call(kernel, out_shape=(jax.ShapeDtypeStruct((FEAT, TOK), BF),...  67.9 us
    pallas_call x1, Pallas kernels, body(): pl.pallas_call(finish, out_shape=tuple((jax.ShapeDtypeStruct(part.shape,...  16.1 us
    unnamed x14, local copies, waits for them, and re-layouts  4.51 us

profile of v3, /device:TPU:1, one launch (start us, length us, event | category | flops | bytes accessed | tf_op | source)
XLA Modules:
  0.0 90.5 jit_solution(10977984099898402322)
XLA Ops:
  1.3 0.7 reshape.13.slots_ref
  2.0 0.0 copy-start.4
  2.0 0.7 copy-done.4
  2.6 0.0 copy-start.6
  2.6 0.7 copy-done.6
  3.3 67.9 %expert_backward.1 = (bf16[64,384]{1,0:T(8,128)(2,1)S(1)}, f32[2,384]{1,0:T(2,128)S(1)}, bf16[192,384]{1,0:T(8,128)(2,1)S(1)}, bf16[192,384]{1,0:T(8,128)(2,1)S(1)}, bf16[192,384]{1,0:T(8,128)(2,1)S(1)}) custom-call(s32[1,2]{1,0:T(1,128)S(1)} %copy-done.6, s32[1]{0:T(128)S(6)} %copy.14.count_ref, f32[2,384]{1,0:T(2,128)S(1)} %bitcast.3, ...), custom_call_target="tpu_custom_call" | custom-call | tf_op jit(solution)/shard_map/expert_backward/pallas_call | solution.py:470
  71.2 0.0 copy-start
  71.2 0.6 copy-done
  71.8 0.0 copy-start.1
  71.8 0.7 copy-done.1
  72.5 0.0 copy-start.2
  72.5 0.7 copy-done.2
  73.2 0.0 copy-start.3
  73.2 0.6 copy-done.3
  73.8 0.0 copy-start.5
  73.8 0.6 copy-done.5
  74.4 16.1 %finish.1 = (bf16[64,384]{1,0:T(8,128)(2,1)}, f32[2,384]{1,0:T(2,128)}, bf16[192,384]{1,0:T(8,128)(2,1)}, bf16[192,384]{1,0:T(8,128)(2,1)}, bf16[192,384]{1,0:T(8,128)(2,1)}) custom-call(bf16[64,384]{1,0:T(8,128)(2,1)} %copy-done.3, f32[2,384]{1,0:T(2,128)} %copy-done.5, bf16[192,384]{1,0:T(8,128)(2,1)} %copy-done, bf16[192,384]{1,0:T(8,128)(2,1)} %copy-done.1, ...), custom_call_target="tpu_custom_call" | custom-call | tf_op jit(solution)/shard_map/finish/pallas_call | solution.py:536
Async XLA Ops:
  2.0 0.7 copy-start.4
  2.6 0.7 copy-start.6
  71.2 0.7 copy-start
  71.8 0.7 copy-start.1
  72.5 0.7 copy-start.2
  73.2 0.6 copy-start.3
  73.8 0.6 copy-start.5

commit v4 on v3

--- a/solution.py
+++ b/solution.py
@@ -19,6 +19,7 @@
 SHARD = 192
 FEAT = 64
 CHUNK = 384
+PARTS = 4
 
 DOWN, UP = 0, 1
 HOPS = {(0, DOWN): 4, (0, UP): 3, (1, DOWN): 3, (1, UP): 4, (2, DOWN): 4, (2, UP): 3, (3, DOWN): 3, (3, UP): 4}
@@ -67,18 +68,14 @@
     def z_dev(step):
         return at(zz=lax.rem(z + step, NZ))
 
-    loads = [
-        pltpu.make_async_copy(src, dst, load_sem.at[i])
-        for i, (src, dst) in enumerate(
-            (
-                (tok_hbm, tok),
-                (wg_hbm, wgu.at[:, 0:HID]),
-                (wu_hbm, wgu.at[:, HID : 2 * HID]),
-                (cot_hbm, cot),
-                (wd_hbm, wd),
-            )
-        )
-    ]
+    part_rows = D // PARTS
+    sources = [(tok_hbm, tok), (cot_hbm, cot)]
+    for k in range(PARTS):
+        rows = pl.ds(k * part_rows, part_rows)
+        sources.append((wg_hbm.at[rows], wgu.at[rows, 0:HID]))
+        sources.append((wu_hbm.at[rows], wgu.at[rows, HID : 2 * HID]))
+    sources.append((wd_hbm, wd))
+    loads = [pltpu.make_async_copy(src, dst, load_sem.at[i]) for i, (src, dst) in enumerate(sources)]
     for load in loads:
         load.start()
 
@@ -140,13 +137,6 @@
         rows_t[t, 1] = part[SHARD:]
         return carry
 
-    lax.fori_loop(0, NY, turn_rows, 0)
-
-    @pl.when(colour == 0)
-    def _():
-        pl.semaphore_wait(ready, len(plane))
-
-
     def plain_copy(src, dst, send, recv, device):
         copy = pltpu.make_async_remote_copy(
             src_ref=src, dst_ref=dst, send_sem=send, recv_sem=recv, device_id=device, device_id_type=MESH
@@ -154,14 +144,22 @@
         copy.start()
         return copy
 
+    lax.fori_loop(0, NY, turn_rows, 0)
+    @pl.when(colour == 0)
+    def _():
+        pl.semaphore_wait(ready, len(plane))
+
     mine = pl.ds((NY // 2) * core, NY // 2)
     rows_copy = plain_copy(rows_t.at[mine, other], rows_x.at[mine], xs_sem.at[0], xr_sem.at[0], x_dev)
 
     loads[1].wait()
-    loads[2].wait()
-    f_gu[...] = jnp.dot(rin[...], wgu[...], preferred_element_type=F32)
-    loads[3].wait()
     take_rows(cot, rct)
+    for k in range(PARTS):
+        loads[2 + 2 * k].wait()
+        loads[3 + 2 * k].wait()
+        rows = slice(k * part_rows, (k + 1) * part_rows)
+        product = jnp.dot(rin[:, rows], wgu[rows, :], preferred_element_type=F32)
+        f_gu[...] = product if k == 0 else f_gu[...] + product
 
     def factor_rows(rows):
         column = fac[rows, :]
@@ -243,12 +241,15 @@
             total = total + y_recv[stream, direction, turn].astype(F32)
         return total
 
-    lax.fori_loop(0, 3, down_partial, 0)
-    for stream, direction in ((0, DOWN), (1, UP), (0, UP), (1, DOWN)):
-        first_turn(stream, direction)
-    lax.fori_loop(3, NY, down_partial, 0)
-
-    loads[4].wait()
+    down_partial(0, 0)
+
+    first_turn(0, DOWN)
+    first_turn(1, UP)
+    lax.fori_loop(1, 3, down_partial, 0)
+    first_turn(0, UP)
+    first_turn(1, DOWN)
+
+    loads[2 + 2 * PARTS].wait()
     f_back[...] = jnp.dot(rct[...], wd[...], preferred_element_type=F32)
 
     def second_part(i, carry):
@@ -263,6 +264,7 @@
     lax.fori_loop(0, ROWS // 32, second_part, 0)
 
     dpre_copy = plain_copy(dpre, dpre_x, xs_sem.at[1], xr_sem.at[1], x_dev)
+    lax.fori_loop(3, NY, down_partial, 0)
 
     def gu_partial(i, carry):
         t = dest(i)
@@ -336,15 +338,18 @@
         dx_xl_copy().start()
         dt_xl_copy().start()
 
+    for stream, direction in ((0, DOWN), (1, UP), (0, UP), (1, DOWN)):
+        forward_turn(stream, direction, 2)
     dpre_copy.wait_recv()
     pass_copy.wait_recv()
-    lax.fori_loop(0, 3, gu_partial, 0)
-    for stream, direction in ((2, DOWN), (3, UP), (2, UP), (3, DOWN)):
-        first_turn(stream, direction)
+    gu_partial(0, 0)
+    first_turn(2, DOWN)
+    first_turn(3, UP)
+    lax.fori_loop(1, 3, gu_partial, 0)
+    first_turn(2, UP)
+    first_turn(3, DOWN)
     lax.fori_loop(3, NY, gu_partial, 0)
 
-    for stream, direction in ((0, DOWN), (1, UP), (0, UP), (1, DOWN)):
-        forward_turn(stream, direction, 2)
 
     @pl.when(colour == 0)
     def _():
@@ -451,23 +456,13 @@
         dt_out_copy().wait_send()
 
 
-def finish(*refs):
-    sem = refs[-1]
-    count = len(refs) // 2
-    copies = [pltpu.make_async_copy(refs[i], refs[count + i], sem.at[i]) for i in range(count)]
-    for copy in copies:
-        copy.start()
-    for copy in copies:
-        copy.wait()
-
-
 def body(tokens, cotangent, w_gate, w_up, w_down_t, gate_probs, slot_ids, block_list, block_count):
     smem = pl.BlockSpec(memory_space=pltpu.SMEM)
     vmem = pl.BlockSpec(memory_space=pltpu.VMEM)
     anywhere = pl.BlockSpec(memory_space=pl.ANY)
     dma = pltpu.SemaphoreType.DMA
     shard = (SHARD, HID)
-    partial = pl.pallas_call(
+    gtok, gprob, gg, gu, gd = pl.pallas_call(
         kernel,
         out_shape=(
             jax.ShapeDtypeStruct((FEAT, TOK), BF),
@@ -513,7 +508,7 @@
             pltpu.VMEM((NZ, 8, ROWS), F32),
             pltpu.VMEM((8, ROWS), F32),
             pltpu.VMEM((8, ROWS), F32),
-            dma((5,)),
+            dma((2 * PARTS + 3,)),
             dma((3,)),
             dma((3,)),
             dma((4, 2, 4)),
@@ -533,14 +528,6 @@
         block_list, block_count, gate_probs.T, slot_ids.reshape(1, TOK),
         tokens, cotangent, w_gate, w_up, w_down_t,
     )
-    gtok, gprob, gg, gu, gd = pl.pallas_call(
-        finish,
-        out_shape=tuple(jax.ShapeDtypeStruct(part.shape, part.dtype) for part in partial),
-        in_specs=[anywhere] * 5,
-        out_specs=(anywhere,) * 5,
-        scratch_shapes=[dma((5,))],
-        name="finish",
-    )(*partial)
     return gtok.T, gprob.T, gg, gu, gd
 
 

time: 90.7 us -> 74.6 us (0.82)
  Pallas kernels: 84 us -> 67.9 us
    pallas_call x1 -> x0, Pallas kernels: 16.1 us -> none  [body(): pl.pallas_call(finish, out_shape=tuple((jax.ShapeDtypeStruct(part.shape,...]
    unnamed x14 -> x9, local copies, waits for them, and re-layouts: 4.51 us -> 4.52 us
where the time goes in v4:
time: 74.6 us; the launch traced here: 74.4 us
  Pallas kernels  67.9 us (91%)
  local copies, waits for them, and re-layouts  5.2 us (7%)
  between operations  1.29 us (2%)
    pallas_call x1, Pallas kernels, body(): pl.pallas_call(kernel, out_shape=(jax.ShapeDtypeStruct((FEAT, TOK), BF),...  67.9 us
    unnamed x9, local copies, waits for them, and re-layouts  4.52 us

profile of v4, /device:TPU:1, one launch (start us, length us, event | category | flops | bytes accessed | tf_op | source)
XLA Modules:
  0.0 74.4 jit_solution(9063871826252920942)
XLA Ops:
  1.3 0.7 reshape.13.slots_ref
  2.0 0.0 copy-start
  2.0 0.7 copy-done
  2.6 0.0 copy-start.1
  2.6 0.7 copy-done.1
  3.3 67.9 %expert_backward.1 = (bf16[64,384]{1,0:T(8,128)(2,1)S(1)}, f32[2,384]{1,0:T(2,128)S(1)}, bf16[192,384]{1,0:T(8,128)(2,1)S(1)}, bf16[192,384]{1,0:T(8,128)(2,1)S(1)}, bf16[192,384]{1,0:T(8,128)(2,1)S(1)}) custom-call(s32[1,2]{1,0:T(1,128)S(1)} %copy-done.1, s32[1]{0:T(128)S(6)} %copy.19.count_ref, f32[2,384]{1,0:T(2,128)S(1)} %bitcast.4, ...), custom_call_target="tpu_custom_call" | custom-call | tf_op jit(solution)/shard_map/expert_backward/pallas_call | solution.py:465
  71.2 0.6 copy.20
  71.9 0.6 copy.21
  72.4 0.7 copy.22
  73.1 0.7 copy.23
  73.8 0.7 copy.24
Async XLA Ops:
  2.0 0.7 copy-start
  2.6 0.7 copy-start.1

commit v5 on v4

--- a/solution.py
+++ b/solution.py
@@ -144,7 +144,8 @@
         copy.start()
         return copy
 
-    lax.fori_loop(0, NY, turn_rows, 0)
+    first_half = (NY // 2) * core
+    lax.fori_loop(first_half, first_half + NY // 2, turn_rows, 0)
     @pl.when(colour == 0)
     def _():
         pl.semaphore_wait(ready, len(plane))
@@ -264,8 +265,8 @@
     lax.fori_loop(0, ROWS // 32, second_part, 0)
 
     dpre_copy = plain_copy(dpre, dpre_x, xs_sem.at[1], xr_sem.at[1], x_dev)
-    lax.fori_loop(3, NY, down_partial, 0)
-
+    second_half = (NY // 2) * (1 - core)
+    lax.fori_loop(second_half, second_half + NY // 2, turn_rows, 0)
     def gu_partial(i, carry):
         t = dest(i)
         part = (
@@ -290,6 +291,8 @@
 
     dx_core_copy = plain_copy(dx_own.at[lax.rem(xl + 1 + colour, 2)], dx_core, cs_sem.at[0], cr_sem.at[0], core_dev)
     dt_core_copy = plain_copy(dt_own, dt_core, cs_sem.at[1], cr_sem.at[1], core_dev)
+
+    lax.fori_loop(3, NY, down_partial, 0)
 
     rows_copy.wait_recv()
     theirs = rows_x.at[mine]
@@ -348,9 +351,6 @@
     lax.fori_loop(1, 3, gu_partial, 0)
     first_turn(2, UP)
     first_turn(3, DOWN)
-    lax.fori_loop(3, NY, gu_partial, 0)
-
-
     @pl.when(colour == 0)
     def _():
         dx_xl_copy().wait_recv()
@@ -372,6 +372,9 @@
             return carry
 
         lax.fori_loop(1, NZ, z_start, 0)
+
+    lax.fori_loop(3, NY, gu_partial, 0)
+
 
     forward_turn(0, DOWN, 3)
     forward_turn(1, UP, 3)

time: 74.6 us -> 74.2 us (level)
  no operation moved by 1% of the time
where the time goes in v5:
time: 74.2 us; the launch traced here: 74 us
  Pallas kernels  67.5 us (91%)
  local copies, waits for them, and re-layouts  5.2 us (7%)
  between operations  1.29 us (2%)
    pallas_call x1, Pallas kernels, body(): pl.pallas_call(kernel, out_shape=(jax.ShapeDtypeStruct((FEAT, TOK), BF),...  67.5 us
    unnamed x9, local copies, waits for them, and re-layouts  4.52 us

profile of v5, /device:TPU:1, one launch (start us, length us, event | category | flops | bytes accessed | tf_op | source)
XLA Modules:
  0.0 74.0 jit_solution(8683060414524675675)
XLA Ops:
  1.3 0.7 reshape.13.slots_ref
  2.0 0.0 copy-start
  2.0 0.7 copy-done
  2.6 0.0 copy-start.1
  2.6 0.7 copy-done.1
  3.3 67.5 %expert_backward.1 = (bf16[64,384]{1,0:T(8,128)(2,1)S(1)}, f32[2,384]{1,0:T(2,128)S(1)}, bf16[192,384]{1,0:T(8,128)(2,1)S(1)}, bf16[192,384]{1,0:T(8,128)(2,1)S(1)}, bf16[192,384]{1,0:T(8,128)(2,1)S(1)}) custom-call(s32[1,2]{1,0:T(1,128)S(1)} %copy-done.1, s32[1]{0:T(128)S(6)} %copy.19.count_ref, f32[2,384]{1,0:T(2,128)S(1)} %bitcast.4, ...), custom_call_target="tpu_custom_call" | custom-call | tf_op jit(solution)/shard_map/expert_backward/pallas_call | solution.py:468
  70.8 0.6 copy.20
  71.4 0.6 copy.21
  72.0 0.7 copy.22
  72.7 0.7 copy.23
  73.3 0.7 copy.24
Async XLA Ops:
  2.0 0.7 copy-start
  2.6 0.7 copy-start.1

commit v6 on v5

--- a/solution.py
+++ b/solution.py
@@ -246,9 +246,6 @@
 
     first_turn(0, DOWN)
     first_turn(1, UP)
-    lax.fori_loop(1, 3, down_partial, 0)
-    first_turn(0, UP)
-    first_turn(1, DOWN)
 
     loads[2 + 2 * PARTS].wait()
     f_back[...] = jnp.dot(rct[...], wd[...], preferred_element_type=F32)
@@ -265,6 +262,9 @@
     lax.fori_loop(0, ROWS // 32, second_part, 0)
 
     dpre_copy = plain_copy(dpre, dpre_x, xs_sem.at[1], xr_sem.at[1], x_dev)
+    lax.fori_loop(1, 3, down_partial, 0)
+    first_turn(0, UP)
+    first_turn(1, DOWN)
     second_half = (NY // 2) * (1 - core)
     lax.fori_loop(second_half, second_half + NY // 2, turn_rows, 0)
     def gu_partial(i, carry):

time: 74.2 us -> 74.2 us (level)
  no operation moved by 1% of the time
where the time goes in v6:
time: 74.2 us; the launch traced here: 74 us
  Pallas kernels  67.5 us (91%)
  local copies, waits for them, and re-layouts  5.2 us (7%)
  between operations  1.29 us (2%)
    pallas_call x1, Pallas kernels, body(): pl.pallas_call(kernel, out_shape=(jax.ShapeDtypeStruct((FEAT, TOK), BF),...  67.5 us
    unnamed x9, local copies, waits for them, and re-layouts  4.52 us

profile of v6, /device:TPU:1, one launch (start us, length us, event | category | flops | bytes accessed | tf_op | source)
XLA Modules:
  0.0 74.0 jit_solution(2949822738955214710)
XLA Ops:
  1.3 0.7 reshape.13.slots_ref
  2.0 0.0 copy-start
  2.0 0.7 copy-done
  2.6 0.0 copy-start.1
  2.6 0.7 copy-done.1
  3.3 67.5 %expert_backward.1 = (bf16[64,384]{1,0:T(8,128)(2,1)S(1)}, f32[2,384]{1,0:T(2,128)S(1)}, bf16[192,384]{1,0:T(8,128)(2,1)S(1)}, bf16[192,384]{1,0:T(8,128)(2,1)S(1)}, bf16[192,384]{1,0:T(8,128)(2,1)S(1)}) custom-call(s32[1,2]{1,0:T(1,128)S(1)} %copy-done.1, s32[1]{0:T(128)S(6)} %copy.19.count_ref, f32[2,384]{1,0:T(2,128)S(1)} %bitcast.4, ...), custom_call_target="tpu_custom_call" | custom-call | tf_op jit(solution)/shard_map/expert_backward/pallas_call | solution.py:468
  70.8 0.6 copy.20
  71.4 0.6 copy.21
  72.0 0.7 copy.22
  72.7 0.7 copy.23
  73.3 0.7 copy.24
Async XLA Ops:
  2.0 0.7 copy-start
  2.6 0.7 copy-start.1
